TPU v7x, 512 devices: a whole 4x8x8 slice. The times are simulated.
512 devices in a mesh: row: 16 (over y, core), col: 4 (over z_hi), height: 8 (over x, z_lo).
Axes of the slice: x: 4, y: 8, z: 8 (z_hi: 4, z_lo: 2; z = z_hi * 2 + z_lo), core: 2. Of those that a mesh axis runs over, the one named last changes fastest.
Arguments:
- impedance: bfloat16 [16, 4, 8, 1536, 1536], P('row', 'col', 'height'), may hold values from -0.125 to 0.125
- sources: bfloat16 [16, 4, 8, 48, 1536], P('row', 'col', 'height'), may hold values from -6 to 6
- coupling: int32 [16, 4, 8, 6], P('row', 'col', 'height'), may hold values 0 or 1
Outputs:
- outgoing: bfloat16 [16, 4, 8, 48, 1536], P('row', 'col', 'height')
Inputs may be any that keep to these rules, and one draw needn't show every extreme that they name: `coupling`: 1 marks a coupled face, 0 an absorbing one.
All inputs are finite; a program needn't handle non-finite values. No bound on the sum of `coupling` on one device may be relied on, other than what follows from the above.
Results may differ from a plain program's by a relative error of at most 0.014.
Values may be sent and summed in bfloat16 or wider, within the bound.
A program may use at most 64 MiB of HBM per device.

v0:
```python
import jax
import jax.numpy as jnp
from jax import lax
from jax.sharding import PartitionSpec as P

ITERS = 8


def from_behind(value, axis, steps):
    count = lax.axis_size(axis)
    leading, last = (max(0, -steps), min(count, count - steps))
    return lax.ppermute(value, axis, [(source, source + steps) for source in range(leading, last)])


def couple(low_face, high_face, axis_pos):
    if axis_pos == 0:
        return (from_behind(high_face, "row", 1), from_behind(low_face, "row", -1))
    if axis_pos == 1:
        return (from_behind(high_face, "col", 1), from_behind(low_face, "col", -1))
    return (from_behind(high_face, "height", 1), from_behind(low_face, "height", -1))


def shards(impedance, sources, coupling):
    square = impedance[0, 0, 0]
    excite = sources[0, 0, 0]
    couple_gain = coupling[0, 0, 0].astype(jnp.bfloat16)
    face_len = square.shape[0] // 6
    incoming = jnp.zeros(excite.shape, jnp.bfloat16)
    outgoing = incoming
    for iteration in range(ITERS):
        driven = (incoming.astype(jnp.float32) + excite.astype(jnp.float32)).astype(jnp.bfloat16)
        sending = iteration + 1 < ITERS
        received = []
        outgoing = jnp.dot(driven, square, preferred_element_type=jnp.float32).astype(jnp.bfloat16)
        if sending:
            for axis_pos in range(3):
                low_face = outgoing[:, 2 * axis_pos * face_len : (2 * axis_pos + 1) * face_len]
                high_face = outgoing[
                    :, (2 * axis_pos + 1) * face_len : (2 * axis_pos + 2) * face_len
                ]
                from_below, from_above = couple(low_face, high_face, axis_pos)
                received.append(from_below)
                received.append(from_above)
        if sending:
            incoming = jnp.concatenate(
                [received[index] * couple_gain[index] for index in range(6)], axis=1
            )
    return outgoing[None, None, None]


def solution(mesh):
    placed = (
        P("row", "col", "height", None, None),
        P("row", "col", "height", None, None),
        P("row", "col", "height", None),
    )
    return jax.shard_map(
        shards,
        mesh=mesh,
        in_specs=placed,
        out_specs=P("row", "col", "height", None, None),
        check_vma=False,
    )
```

profile of v0, /device:TPU:25, one launch (start us, length us, event | category | flops | bytes accessed | tf_op | source)
XLA Modules:
  0.0 218.0 jit_solution(4514130615436974875)
XLA Ops:
  0.0 3.5 %fusion.16 = bf16[48,1536]{1,0:T(8,128)(2,1)S(1)} fusion(bf16[1,1,1,1536,1536]{4,3,2,1,0:T(8,128)(2,1)} %param.3, bf16[1,1,1,48,1536]{4,3,2,1,0:T(8,128)(2,1)} %param.4), kind=kOutput, calls=%fused_computation.16 | convolution fusion | flops 226566144 | bytes 5013504 | tf_op jit(solution)/shard_map/dot_general | solution.py:34
  4.8 4.6 %collective-permute-start.4 = (bf16[48,256]{1,0:T(8,128)(2,1)S(1)}, bf16[48,256]{1,0:T(8,128)(2,1)S(1)}, u32[]{:S(2)}, u32[]{:S(2)}) collective-permute-start(bf16[48,256]{1,0:T(8,128)(2,1)S(1)} %get-tuple-element.42), channel_id=1, source_target_pairs={{0,1},{1,2},{2,3},{3,4},{4,5},{5,6},{6,7},{8,9},{9,10},{10,11},{11... | collective-permute-start | bytes 73736 | tf_op jit(solution)/shard_map/ppermute | solution.py:12
  10.7 6.4 %collective-permute-start.2 = (bf16[48,256]{1,0:T(8,128)(2,1)S(1)}, bf16[48,256]{1,0:T(8,128)(2,1)S(1)}, u32[]{:S(2)}, u32[]{:S(2)}) collective-permute-start(bf16[48,256]{1,0:T(8,128)(2,1)S(1)} %get-tuple-element.44), channel_id=1, source_target_pairs={{0,8},{8,16},{16,24},{1,9},{9,17},{17,25},{2,10},{10,18},{18,26},{... | collective-permute-start | bytes 73736 | tf_op jit(solution)/shard_map/ppermute | solution.py:12
  17.2 5.5 %collective-permute-start = (bf16[48,256]{1,0:T(8,128)(2,1)S(1)}, bf16[48,256]{1,0:T(8,128)(2,1)S(1)}, u32[]{:S(2)}, u32[]{:S(2)}) collective-permute-start(bf16[48,256]{1,0:T(8,128)(2,1)S(1)} %get-tuple-element.46), channel_id=1, source_target_pairs={{0,32},{32,64},{64,96},{96,128},{128,160},{160,192},{192,224},{224... | collective-permute-start | bytes 73736 | tf_op jit(solution)/shard_map/ppermute | solution.py:12
  26.2 4.4 %collective-permute-done.1 = bf16[48,256]{1,0:T(8,128)(2,1)S(1)} collective-permute-done((bf16[48,256]{1,0:T(8,128)(2,1)S(1)}, bf16[48,256]{1,0:T(8,128)(2,1)S(1)}, u32[]{:S(2)}, u32[]{:S(2)}) %collective-permute-start.1) | collective-permute-done | bytes 24608 | tf_op jit(solution)/shard_map/ppermute | solution.py:12
  39.6 5.2 %collective-permute-start.10 = (bf16[48,256]{1,0:T(8,128)(2,1)S(1)}, bf16[48,256]{1,0:T(8,128)(2,1)S(1)}, u32[]{:S(2)}, u32[]{:S(2)}) collective-permute-start(bf16[48,256]{1,0:T(8,128)(2,1)S(1)} %get-tuple-element.36), channel_id=1, source_target_pairs={{0,1},{1,2},{2,3},{3,4},{4,5},{5,6},{6,7},{8,9},{9,10},{10,11},{11... | collective-permute-start | bytes 73736 | tf_op jit(solution)/shard_map/ppermute | solution.py:12
  46.1 6.7 %collective-permute-start.8 = (bf16[48,256]{1,0:T(8,128)(2,1)S(1)}, bf16[48,256]{1,0:T(8,128)(2,1)S(1)}, u32[]{:S(2)}, u32[]{:S(2)}) collective-permute-start(bf16[48,256]{1,0:T(8,128)(2,1)S(1)} %get-tuple-element.38), channel_id=1, source_target_pairs={{0,8},{8,16},{16,24},{1,9},{9,17},{17,25},{2,10},{10,18},{18,26},{... | collective-permute-start | bytes 73736 | tf_op jit(solution)/shard_map/ppermute | solution.py:12
  52.8 3.0 %collective-permute-start.7 = (bf16[48,256]{1,0:T(8,128)(2,1)S(1)}, bf16[48,256]{1,0:T(8,128)(2,1)S(1)}, u32[]{:S(2)}, u32[]{:S(2)}) collective-permute-start(bf16[48,256]{1,0:T(8,128)(2,1)S(1)} %get-tuple-element.39), channel_id=1, source_target_pairs={{32,0},{64,32},{96,64},{128,96},{160,128},{192,160},{224,192},{256... | collective-permute-start | bytes 73736 | tf_op jit(solution)/shard_map/ppermute | solution.py:12
  57.0 2.2 %collective-permute-done.7 = bf16[48,256]{1,0:T(8,128)(2,1)S(1)} collective-permute-done((bf16[48,256]{1,0:T(8,128)(2,1)S(1)}, bf16[48,256]{1,0:T(8,128)(2,1)S(1)}, u32[]{:S(2)}, u32[]{:S(2)}) %collective-permute-start.7) | collective-permute-done | bytes 24608 | tf_op jit(solution)/shard_map/ppermute | solution.py:12
  70.5 4.9 %collective-permute-start.16 = (bf16[48,256]{1,0:T(8,128)(2,1)S(1)}, bf16[48,256]{1,0:T(8,128)(2,1)S(1)}, u32[]{:S(2)}, u32[]{:S(2)}) collective-permute-start(bf16[48,256]{1,0:T(8,128)(2,1)S(1)} %get-tuple-element.30), channel_id=1, source_target_pairs={{0,1},{1,2},{2,3},{3,4},{4,5},{5,6},{6,7},{8,9},{9,10},{10,11},{11... | collective-permute-start | bytes 73736 | tf_op jit(solution)/shard_map/ppermute | solution.py:12
  76.7 6.1 %collective-permute-start.14 = (bf16[48,256]{1,0:T(8,128)(2,1)S(1)}, bf16[48,256]{1,0:T(8,128)(2,1)S(1)}, u32[]{:S(2)}, u32[]{:S(2)}) collective-permute-start(bf16[48,256]{1,0:T(8,128)(2,1)S(1)} %get-tuple-element.32), channel_id=1, source_target_pairs={{0,8},{8,16},{16,24},{1,9},{9,17},{17,25},{2,10},{10,18},{18,26},{... | collective-permute-start | bytes 73736 | tf_op jit(solution)/shard_map/ppermute | solution.py:12
  82.8 3.0 %collective-permute-start.13 = (bf16[48,256]{1,0:T(8,128)(2,1)S(1)}, bf16[48,256]{1,0:T(8,128)(2,1)S(1)}, u32[]{:S(2)}, u32[]{:S(2)}) collective-permute-start(bf16[48,256]{1,0:T(8,128)(2,1)S(1)} %get-tuple-element.33), channel_id=1, source_target_pairs={{32,0},{64,32},{96,64},{128,96},{160,128},{192,160},{224,192},{256... | collective-permute-start | bytes 73736 | tf_op jit(solution)/shard_map/ppermute | solution.py:12
  87.0 2.2 %collective-permute-done.13 = bf16[48,256]{1,0:T(8,128)(2,1)S(1)} collective-permute-done((bf16[48,256]{1,0:T(8,128)(2,1)S(1)}, bf16[48,256]{1,0:T(8,128)(2,1)S(1)}, u32[]{:S(2)}, u32[]{:S(2)}) %collective-permute-start.13) | collective-permute-done | bytes 24608 | tf_op jit(solution)/shard_map/ppermute | solution.py:12
  97.3 1.9 collective-permute-start.18
  100.5 4.9 %collective-permute-start.22 = (bf16[48,256]{1,0:T(8,128)(2,1)S(1)}, bf16[48,256]{1,0:T(8,128)(2,1)S(1)}, u32[]{:S(2)}, u32[]{:S(2)}) collective-permute-start(bf16[48,256]{1,0:T(8,128)(2,1)S(1)} %get-tuple-element.24), channel_id=1, source_target_pairs={{0,1},{1,2},{2,3},{3,4},{4,5},{5,6},{6,7},{8,9},{9,10},{10,11},{11... | collective-permute-start | bytes 73736 | tf_op jit(solution)/shard_map/ppermute | solution.py:12
  106.7 6.1 %collective-permute-start.20 = (bf16[48,256]{1,0:T(8,128)(2,1)S(1)}, bf16[48,256]{1,0:T(8,128)(2,1)S(1)}, u32[]{:S(2)}, u32[]{:S(2)}) collective-permute-start(bf16[48,256]{1,0:T(8,128)(2,1)S(1)} %get-tuple-element.26), channel_id=1, source_target_pairs={{0,8},{8,16},{16,24},{1,9},{9,17},{17,25},{2,10},{10,18},{18,26},{... | collective-permute-start | bytes 73736 | tf_op jit(solution)/shard_map/ppermute | solution.py:12
  112.8 3.0 %collective-permute-start.19 = (bf16[48,256]{1,0:T(8,128)(2,1)S(1)}, bf16[48,256]{1,0:T(8,128)(2,1)S(1)}, u32[]{:S(2)}, u32[]{:S(2)}) collective-permute-start(bf16[48,256]{1,0:T(8,128)(2,1)S(1)} %get-tuple-element.27), channel_id=1, source_target_pairs={{32,0},{64,32},{96,64},{128,96},{160,128},{192,160},{224,192},{256... | collective-permute-start | bytes 73736 | tf_op jit(solution)/shard_map/ppermute | solution.py:12
  117.0 2.2 %collective-permute-done.19 = bf16[48,256]{1,0:T(8,128)(2,1)S(1)} collective-permute-done((bf16[48,256]{1,0:T(8,128)(2,1)S(1)}, bf16[48,256]{1,0:T(8,128)(2,1)S(1)}, u32[]{:S(2)}, u32[]{:S(2)}) %collective-permute-start.19) | collective-permute-done | bytes 24608 | tf_op jit(solution)/shard_map/ppermute | solution.py:12
  130.5 4.9 %collective-permute-start.28 = (bf16[48,256]{1,0:T(8,128)(2,1)S(1)}, bf16[48,256]{1,0:T(8,128)(2,1)S(1)}, u32[]{:S(2)}, u32[]{:S(2)}) collective-permute-start(bf16[48,256]{1,0:T(8,128)(2,1)S(1)} %get-tuple-element.18), channel_id=1, source_target_pairs={{0,1},{1,2},{2,3},{3,4},{4,5},{5,6},{6,7},{8,9},{9,10},{10,11},{11... | collective-permute-start | bytes 73736 | tf_op jit(solution)/shard_map/ppermute | solution.py:12
  136.7 6.1 %collective-permute-start.26 = (bf16[48,256]{1,0:T(8,128)(2,1)S(1)}, bf16[48,256]{1,0:T(8,128)(2,1)S(1)}, u32[]{:S(2)}, u32[]{:S(2)}) collective-permute-start(bf16[48,256]{1,0:T(8,128)(2,1)S(1)} %get-tuple-element.20), channel_id=1, source_target_pairs={{0,8},{8,16},{16,24},{1,9},{9,17},{17,25},{2,10},{10,18},{18,26},{... | collective-permute-start | bytes 73736 | tf_op jit(solution)/shard_map/ppermute | solution.py:12
  142.8 3.0 %collective-permute-start.25 = (bf16[48,256]{1,0:T(8,128)(2,1)S(1)}, bf16[48,256]{1,0:T(8,128)(2,1)S(1)}, u32[]{:S(2)}, u32[]{:S(2)}) collective-permute-start(bf16[48,256]{1,0:T(8,128)(2,1)S(1)} %get-tuple-element.21), channel_id=1, source_target_pairs={{32,0},{64,32},{96,64},{128,96},{160,128},{192,160},{224,192},{256... | collective-permute-start | bytes 73736 | tf_op jit(solution)/shard_map/ppermute | solution.py:12
  147.0 2.2 %collective-permute-done.25 = bf16[48,256]{1,0:T(8,128)(2,1)S(1)} collective-permute-done((bf16[48,256]{1,0:T(8,128)(2,1)S(1)}, bf16[48,256]{1,0:T(8,128)(2,1)S(1)}, u32[]{:S(2)}, u32[]{:S(2)}) %collective-permute-start.25) | collective-permute-done | bytes 24608 | tf_op jit(solution)/shard_map/ppermute | solution.py:12
  160.5 4.9 %collective-permute-start.34 = (bf16[48,256]{1,0:T(8,128)(2,1)S(1)}, bf16[48,256]{1,0:T(8,128)(2,1)S(1)}, u32[]{:S(2)}, u32[]{:S(2)}) collective-permute-start(bf16[48,256]{1,0:T(8,128)(2,1)S(1)} %get-tuple-element.12), channel_id=1, source_target_pairs={{0,1},{1,2},{2,3},{3,4},{4,5},{5,6},{6,7},{8,9},{9,10},{10,11},{11... | collective-permute-start | bytes 73736 | tf_op jit(solution)/shard_map/ppermute | solution.py:12
  166.7 6.1 %collective-permute-start.32 = (bf16[48,256]{1,0:T(8,128)(2,1)S(1)}, bf16[48,256]{1,0:T(8,128)(2,1)S(1)}, u32[]{:S(2)}, u32[]{:S(2)}) collective-permute-start(bf16[48,256]{1,0:T(8,128)(2,1)S(1)} %get-tuple-element.14), channel_id=1, source_target_pairs={{0,8},{8,16},{16,24},{1,9},{9,17},{17,25},{2,10},{10,18},{18,26},{... | collective-permute-start | bytes 73736 | tf_op jit(solution)/shard_map/ppermute | solution.py:12
  172.8 3.0 %collective-permute-start.31 = (bf16[48,256]{1,0:T(8,128)(2,1)S(1)}, bf16[48,256]{1,0:T(8,128)(2,1)S(1)}, u32[]{:S(2)}, u32[]{:S(2)}) collective-permute-start(bf16[48,256]{1,0:T(8,128)(2,1)S(1)} %get-tuple-element.15), channel_id=1, source_target_pairs={{32,0},{64,32},{96,64},{128,96},{160,128},{192,160},{224,192},{256... | collective-permute-start | bytes 73736 | tf_op jit(solution)/shard_map/ppermute | solution.py:12
  177.0 2.2 %collective-permute-done.31 = bf16[48,256]{1,0:T(8,128)(2,1)S(1)} collective-permute-done((bf16[48,256]{1,0:T(8,128)(2,1)S(1)}, bf16[48,256]{1,0:T(8,128)(2,1)S(1)}, u32[]{:S(2)}, u32[]{:S(2)}) %collective-permute-start.31) | collective-permute-done | bytes 24608 | tf_op jit(solution)/shard_map/ppermute | solution.py:12
  187.3 1.9 collective-permute-start.36
  190.5 4.9 %collective-permute-start.40 = (bf16[48,256]{1,0:T(8,128)(2,1)S(1)}, bf16[48,256]{1,0:T(8,128)(2,1)S(1)}, u32[]{:S(2)}, u32[]{:S(2)}) collective-permute-start(bf16[48,256]{1,0:T(8,128)(2,1)S(1)} %get-tuple-element.6), channel_id=1, source_target_pairs={{0,1},{1,2},{2,3},{3,4},{4,5},{5,6},{6,7},{8,9},{9,10},{10,11},{11... | collective-permute-start | bytes 73736 | tf_op jit(solution)/shard_map/ppermute | solution.py:12
  196.7 6.1 %collective-permute-start.38 = (bf16[48,256]{1,0:T(8,128)(2,1)S(1)}, bf16[48,256]{1,0:T(8,128)(2,1)S(1)}, u32[]{:S(2)}, u32[]{:S(2)}) collective-permute-start(bf16[48,256]{1,0:T(8,128)(2,1)S(1)} %get-tuple-element.8), channel_id=1, source_target_pairs={{0,8},{8,16},{16,24},{1,9},{9,17},{17,25},{2,10},{10,18},{18,26},{... | collective-permute-start | bytes 73736 | tf_op jit(solution)/shard_map/ppermute | solution.py:12
  202.8 3.0 %collective-permute-start.37 = (bf16[48,256]{1,0:T(8,128)(2,1)S(1)}, bf16[48,256]{1,0:T(8,128)(2,1)S(1)}, u32[]{:S(2)}, u32[]{:S(2)}) collective-permute-start(bf16[48,256]{1,0:T(8,128)(2,1)S(1)} %get-tuple-element.9), channel_id=1, source_target_pairs={{32,0},{64,32},{96,64},{128,96},{160,128},{192,160},{224,192},{256... | collective-permute-start | bytes 73736 | tf_op jit(solution)/shard_map/ppermute | solution.py:12
  207.0 2.2 %collective-permute-done.37 = bf16[48,256]{1,0:T(8,128)(2,1)S(1)} collective-permute-done((bf16[48,256]{1,0:T(8,128)(2,1)S(1)}, bf16[48,256]{1,0:T(8,128)(2,1)S(1)}, u32[]{:S(2)}, u32[]{:S(2)}) %collective-permute-start.37) | collective-permute-done | bytes 24608 | tf_op jit(solution)/shard_map/ppermute | solution.py:12
  215.5 2.4 %fusion.40 = bf16[1,1,1,48,1536]{4,3,2,1,0:T(8,128)(2,1)} fusion(bf16[1,1,1,1536,1536]{4,3,2,1,0:T(8,128)(2,1)S(1)} %copy-done, bf16[1,1,1,48,1536]{4,3,2,1,0:T(8,128)(2,1)S(1)} %copy-done.1, bf16[1,1,1,48,1536]{4,3,2,1,0:T(8,128)(2,1)} %constant_dynamic-update-slice_fusion.36), kind=kOutput, calls=%fused_computation.24 | convolution fusion | flops 226861056 | bytes 5160960 | tf_op jit(solution)/shard_map/dot_general | solution.py:34
  (119 shorter events, 88.7 us)
Async XLA Ops:
  3.5 29.7 %collective-permute-start.5 = (bf16[48,256]{1,0:T(8,128)(2,1)S(1)}, bf16[48,256]{1,0:T(8,128)(2,1)S(1)}, u32[]{:S(2)}, u32[]{:S(2)}) collective-permute-start(bf16[48,256]{1,0:T(8,128)(2,1)S(1)} %get-tuple-element.41), channel_id=1, source_target_pairs={{1,0},{2,1},{3,2},{4,3},{5,4},{6,5},{7,6},{9,8},{10,9},{11,10},{12... | collective-permute-start | bytes 73736 | tf_op jit(solution)/shard_map/ppermute | solution.py:12
  4.8 27.7 %collective-permute-start.4 = (bf16[48,256]{1,0:T(8,128)(2,1)S(1)}, bf16[48,256]{1,0:T(8,128)(2,1)S(1)}, u32[]{:S(2)}, u32[]{:S(2)}) collective-permute-start(bf16[48,256]{1,0:T(8,128)(2,1)S(1)} %get-tuple-element.42), channel_id=1, source_target_pairs={{0,1},{1,2},{2,3},{3,4},{4,5},{5,6},{6,7},{8,9},{9,10},{10,11},{11... | collective-permute-start | bytes 73736 | tf_op jit(solution)/shard_map/ppermute | solution.py:12
  9.4 22.4 %collective-permute-start.3 = (bf16[48,256]{1,0:T(8,128)(2,1)S(1)}, bf16[48,256]{1,0:T(8,128)(2,1)S(1)}, u32[]{:S(2)}, u32[]{:S(2)}) collective-permute-start(bf16[48,256]{1,0:T(8,128)(2,1)S(1)} %get-tuple-element.43), channel_id=1, source_target_pairs={{8,0},{16,8},{24,16},{9,1},{17,9},{25,17},{10,2},{18,10},{26,18},{... | collective-permute-start | bytes 73736 | tf_op jit(solution)/shard_map/ppermute | solution.py:12
  10.7 20.5 %collective-permute-start.2 = (bf16[48,256]{1,0:T(8,128)(2,1)S(1)}, bf16[48,256]{1,0:T(8,128)(2,1)S(1)}, u32[]{:S(2)}, u32[]{:S(2)}) collective-permute-start(bf16[48,256]{1,0:T(8,128)(2,1)S(1)} %get-tuple-element.44), channel_id=1, source_target_pairs={{0,8},{8,16},{16,24},{1,9},{9,17},{17,25},{2,10},{10,18},{18,26},{... | collective-permute-start | bytes 73736 | tf_op jit(solution)/shard_map/ppermute | solution.py:12
  36.4 16.5 %collective-permute-start.6 = (bf16[48,256]{1,0:T(8,128)(2,1)S(1)}, bf16[48,256]{1,0:T(8,128)(2,1)S(1)}, u32[]{:S(2)}, u32[]{:S(2)}) collective-permute-start(bf16[48,256]{1,0:T(8,128)(2,1)S(1)} %get-tuple-element.40), channel_id=1, source_target_pairs={{0,32},{32,64},{64,96},{96,128},{128,160},{160,192},{192,224},{224... | collective-permute-start | bytes 73736 | tf_op jit(solution)/shard_map/ppermute | solution.py:12
  38.3 25.9 %collective-permute-start.11 = (bf16[48,256]{1,0:T(8,128)(2,1)S(1)}, bf16[48,256]{1,0:T(8,128)(2,1)S(1)}, u32[]{:S(2)}, u32[]{:S(2)}) collective-permute-start(bf16[48,256]{1,0:T(8,128)(2,1)S(1)} %get-tuple-element.35), channel_id=1, source_target_pairs={{1,0},{2,1},{3,2},{4,3},{5,4},{6,5},{7,6},{9,8},{10,9},{11,10},{12... | collective-permute-start | bytes 73736 | tf_op jit(solution)/shard_map/ppermute | solution.py:12
  39.6 23.3 %collective-permute-start.10 = (bf16[48,256]{1,0:T(8,128)(2,1)S(1)}, bf16[48,256]{1,0:T(8,128)(2,1)S(1)}, u32[]{:S(2)}, u32[]{:S(2)}) collective-permute-start(bf16[48,256]{1,0:T(8,128)(2,1)S(1)} %get-tuple-element.36), channel_id=1, source_target_pairs={{0,1},{1,2},{2,3},{3,4},{4,5},{5,6},{6,7},{8,9},{9,10},{10,11},{11... | collective-permute-start | bytes 73736 | tf_op jit(solution)/shard_map/ppermute | solution.py:12
  44.8 16.9 %collective-permute-start.9 = (bf16[48,256]{1,0:T(8,128)(2,1)S(1)}, bf16[48,256]{1,0:T(8,128)(2,1)S(1)}, u32[]{:S(2)}, u32[]{:S(2)}) collective-permute-start(bf16[48,256]{1,0:T(8,128)(2,1)S(1)} %get-tuple-element.37), channel_id=1, source_target_pairs={{8,0},{16,8},{24,16},{9,1},{17,9},{25,17},{10,2},{18,10},{26,18},{... | collective-permute-start | bytes 73736 | tf_op jit(solution)/shard_map/ppermute | solution.py:12
  46.1 14.4 %collective-permute-start.8 = (bf16[48,256]{1,0:T(8,128)(2,1)S(1)}, bf16[48,256]{1,0:T(8,128)(2,1)S(1)}, u32[]{:S(2)}, u32[]{:S(2)}) collective-permute-start(bf16[48,256]{1,0:T(8,128)(2,1)S(1)} %get-tuple-element.38), channel_id=1, source_target_pairs={{0,8},{8,16},{16,24},{1,9},{9,17},{17,25},{2,10},{10,18},{18,26},{... | collective-permute-start | bytes 73736 | tf_op jit(solution)/shard_map/ppermute | solution.py:12
  67.3 15.5 %collective-permute-start.12 = (bf16[48,256]{1,0:T(8,128)(2,1)S(1)}, bf16[48,256]{1,0:T(8,128)(2,1)S(1)}, u32[]{:S(2)}, u32[]{:S(2)}) collective-permute-start(bf16[48,256]{1,0:T(8,128)(2,1)S(1)} %get-tuple-element.34), channel_id=1, source_target_pairs={{0,32},{32,64},{64,96},{96,128},{128,160},{160,192},{192,224},{224... | collective-permute-start | bytes 73736 | tf_op jit(solution)/shard_map/ppermute | solution.py:12
  69.2 25.0 %collective-permute-start.17 = (bf16[48,256]{1,0:T(8,128)(2,1)S(1)}, bf16[48,256]{1,0:T(8,128)(2,1)S(1)}, u32[]{:S(2)}, u32[]{:S(2)}) collective-permute-start(bf16[48,256]{1,0:T(8,128)(2,1)S(1)} %get-tuple-element.29), channel_id=1, source_target_pairs={{1,0},{2,1},{3,2},{4,3},{5,4},{6,5},{7,6},{9,8},{10,9},{11,10},{12... | collective-permute-start | bytes 73736 | tf_op jit(solution)/shard_map/ppermute | solution.py:12
  70.5 22.4 %collective-permute-start.16 = (bf16[48,256]{1,0:T(8,128)(2,1)S(1)}, bf16[48,256]{1,0:T(8,128)(2,1)S(1)}, u32[]{:S(2)}, u32[]{:S(2)}) collective-permute-start(bf16[48,256]{1,0:T(8,128)(2,1)S(1)} %get-tuple-element.30), channel_id=1, source_target_pairs={{0,1},{1,2},{2,3},{3,4},{4,5},{5,6},{6,7},{8,9},{9,10},{10,11},{11... | collective-permute-start | bytes 73736 | tf_op jit(solution)/shard_map/ppermute | solution.py:12
  75.4 16.3 %collective-permute-start.15 = (bf16[48,256]{1,0:T(8,128)(2,1)S(1)}, bf16[48,256]{1,0:T(8,128)(2,1)S(1)}, u32[]{:S(2)}, u32[]{:S(2)}) collective-permute-start(bf16[48,256]{1,0:T(8,128)(2,1)S(1)} %get-tuple-element.31), channel_id=1, source_target_pairs={{8,0},{16,8},{24,16},{9,1},{17,9},{25,17},{10,2},{18,10},{26,18},{... | collective-permute-start | bytes 73736 | tf_op jit(solution)/shard_map/ppermute | solution.py:12
  76.7 13.7 %collective-permute-start.14 = (bf16[48,256]{1,0:T(8,128)(2,1)S(1)}, bf16[48,256]{1,0:T(8,128)(2,1)S(1)}, u32[]{:S(2)}, u32[]{:S(2)}) collective-permute-start(bf16[48,256]{1,0:T(8,128)(2,1)S(1)} %get-tuple-element.32), channel_id=1, source_target_pairs={{0,8},{8,16},{16,24},{1,9},{9,17},{17,25},{2,10},{10,18},{18,26},{... | collective-permute-start | bytes 73736 | tf_op jit(solution)/shard_map/ppermute | solution.py:12
  97.3 15.5 %collective-permute-start.18 = (bf16[48,256]{1,0:T(8,128)(2,1)S(1)}, bf16[48,256]{1,0:T(8,128)(2,1)S(1)}, u32[]{:S(2)}, u32[]{:S(2)}) collective-permute-start(bf16[48,256]{1,0:T(8,128)(2,1)S(1)} %get-tuple-element.28), channel_id=1, source_target_pairs={{0,32},{32,64},{64,96},{96,128},{128,160},{160,192},{192,224},{224... | collective-permute-start | bytes 73736 | tf_op jit(solution)/shard_map/ppermute | solution.py:12
  99.2 25.0 %collective-permute-start.23 = (bf16[48,256]{1,0:T(8,128)(2,1)S(1)}, bf16[48,256]{1,0:T(8,128)(2,1)S(1)}, u32[]{:S(2)}, u32[]{:S(2)}) collective-permute-start(bf16[48,256]{1,0:T(8,128)(2,1)S(1)} %get-tuple-element.23), channel_id=1, source_target_pairs={{1,0},{2,1},{3,2},{4,3},{5,4},{6,5},{7,6},{9,8},{10,9},{11,10},{12... | collective-permute-start | bytes 73736 | tf_op jit(solution)/shard_map/ppermute | solution.py:12
  100.5 22.3 %collective-permute-start.22 = (bf16[48,256]{1,0:T(8,128)(2,1)S(1)}, bf16[48,256]{1,0:T(8,128)(2,1)S(1)}, u32[]{:S(2)}, u32[]{:S(2)}) collective-permute-start(bf16[48,256]{1,0:T(8,128)(2,1)S(1)} %get-tuple-element.24), channel_id=1, source_target_pairs={{0,1},{1,2},{2,3},{3,4},{4,5},{5,6},{6,7},{8,9},{9,10},{10,11},{11... | collective-permute-start | bytes 73736 | tf_op jit(solution)/shard_map/ppermute | solution.py:12
  105.4 16.3 %collective-permute-start.21 = (bf16[48,256]{1,0:T(8,128)(2,1)S(1)}, bf16[48,256]{1,0:T(8,128)(2,1)S(1)}, u32[]{:S(2)}, u32[]{:S(2)}) collective-permute-start(bf16[48,256]{1,0:T(8,128)(2,1)S(1)} %get-tuple-element.25), channel_id=1, source_target_pairs={{8,0},{16,8},{24,16},{9,1},{17,9},{25,17},{10,2},{18,10},{26,18},{... | collective-permute-start | bytes 73736 | tf_op jit(solution)/shard_map/ppermute | solution.py:12
  106.7 13.7 %collective-permute-start.20 = (bf16[48,256]{1,0:T(8,128)(2,1)S(1)}, bf16[48,256]{1,0:T(8,128)(2,1)S(1)}, u32[]{:S(2)}, u32[]{:S(2)}) collective-permute-start(bf16[48,256]{1,0:T(8,128)(2,1)S(1)} %get-tuple-element.26), channel_id=1, source_target_pairs={{0,8},{8,16},{16,24},{1,9},{9,17},{17,25},{2,10},{10,18},{18,26},{... | collective-permute-start | bytes 73736 | tf_op jit(solution)/shard_map/ppermute | solution.py:12
  127.3 15.5 %collective-permute-start.24 = (bf16[48,256]{1,0:T(8,128)(2,1)S(1)}, bf16[48,256]{1,0:T(8,128)(2,1)S(1)}, u32[]{:S(2)}, u32[]{:S(2)}) collective-permute-start(bf16[48,256]{1,0:T(8,128)(2,1)S(1)} %get-tuple-element.22), channel_id=1, source_target_pairs={{0,32},{32,64},{64,96},{96,128},{128,160},{160,192},{192,224},{224... | collective-permute-start | bytes 73736 | tf_op jit(solution)/shard_map/ppermute | solution.py:12
  129.2 25.0 %collective-permute-start.29 = (bf16[48,256]{1,0:T(8,128)(2,1)S(1)}, bf16[48,256]{1,0:T(8,128)(2,1)S(1)}, u32[]{:S(2)}, u32[]{:S(2)}) collective-permute-start(bf16[48,256]{1,0:T(8,128)(2,1)S(1)} %get-tuple-element.17), channel_id=1, source_target_pairs={{1,0},{2,1},{3,2},{4,3},{5,4},{6,5},{7,6},{9,8},{10,9},{11,10},{12... | collective-permute-start | bytes 73736 | tf_op jit(solution)/shard_map/ppermute | solution.py:12
  130.5 22.4 %collective-permute-start.28 = (bf16[48,256]{1,0:T(8,128)(2,1)S(1)}, bf16[48,256]{1,0:T(8,128)(2,1)S(1)}, u32[]{:S(2)}, u32[]{:S(2)}) collective-permute-start(bf16[48,256]{1,0:T(8,128)(2,1)S(1)} %get-tuple-element.18), channel_id=1, source_target_pairs={{0,1},{1,2},{2,3},{3,4},{4,5},{5,6},{6,7},{8,9},{9,10},{10,11},{11... | collective-permute-start | bytes 73736 | tf_op jit(solution)/shard_map/ppermute | solution.py:12
  135.4 16.3 %collective-permute-start.27 = (bf16[48,256]{1,0:T(8,128)(2,1)S(1)}, bf16[48,256]{1,0:T(8,128)(2,1)S(1)}, u32[]{:S(2)}, u32[]{:S(2)}) collective-permute-start(bf16[48,256]{1,0:T(8,128)(2,1)S(1)} %get-tuple-element.19), channel_id=1, source_target_pairs={{8,0},{16,8},{24,16},{9,1},{17,9},{25,17},{10,2},{18,10},{26,18},{... | collective-permute-start | bytes 73736 | tf_op jit(solution)/shard_map/ppermute | solution.py:12
  157.3 15.5 %collective-permute-start.30 = (bf16[48,256]{1,0:T(8,128)(2,1)S(1)}, bf16[48,256]{1,0:T(8,128)(2,1)S(1)}, u32[]{:S(2)}, u32[]{:S(2)}) collective-permute-start(bf16[48,256]{1,0:T(8,128)(2,1)S(1)} %get-tuple-element.16), channel_id=1, source_target_pairs={{0,32},{32,64},{64,96},{96,128},{128,160},{160,192},{192,224},{224... | collective-permute-start | bytes 73736 | tf_op jit(solution)/shard_map/ppermute | solution.py:12
  159.2 25.0 %collective-permute-start.35 = (bf16[48,256]{1,0:T(8,128)(2,1)S(1)}, bf16[48,256]{1,0:T(8,128)(2,1)S(1)}, u32[]{:S(2)}, u32[]{:S(2)}) collective-permute-start(bf16[48,256]{1,0:T(8,128)(2,1)S(1)} %get-tuple-element.11), channel_id=1, source_target_pairs={{1,0},{2,1},{3,2},{4,3},{5,4},{6,5},{7,6},{9,8},{10,9},{11,10},{12... | collective-permute-start | bytes 73736 | tf_op jit(solution)/shard_map/ppermute | solution.py:12
  160.5 22.4 %collective-permute-start.34 = (bf16[48,256]{1,0:T(8,128)(2,1)S(1)}, bf16[48,256]{1,0:T(8,128)(2,1)S(1)}, u32[]{:S(2)}, u32[]{:S(2)}) collective-permute-start(bf16[48,256]{1,0:T(8,128)(2,1)S(1)} %get-tuple-element.12), channel_id=1, source_target_pairs={{0,1},{1,2},{2,3},{3,4},{4,5},{5,6},{6,7},{8,9},{9,10},{10,11},{11... | collective-permute-start | bytes 73736 | tf_op jit(solution)/shard_map/ppermute | solution.py:12
  165.4 16.3 %collective-permute-start.33 = (bf16[48,256]{1,0:T(8,128)(2,1)S(1)}, bf16[48,256]{1,0:T(8,128)(2,1)S(1)}, u32[]{:S(2)}, u32[]{:S(2)}) collective-permute-start(bf16[48,256]{1,0:T(8,128)(2,1)S(1)} %get-tuple-element.13), channel_id=1, source_target_pairs={{8,0},{16,8},{24,16},{9,1},{17,9},{25,17},{10,2},{18,10},{26,18},{... | collective-permute-start | bytes 73736 | tf_op jit(solution)/shard_map/ppermute | solution.py:12
  187.3 15.5 %collective-permute-start.36 = (bf16[48,256]{1,0:T(8,128)(2,1)S(1)}, bf16[48,256]{1,0:T(8,128)(2,1)S(1)}, u32[]{:S(2)}, u32[]{:S(2)}) collective-permute-start(bf16[48,256]{1,0:T(8,128)(2,1)S(1)} %get-tuple-element.10), channel_id=1, source_target_pairs={{0,32},{32,64},{64,96},{96,128},{128,160},{160,192},{192,224},{224... | collective-permute-start | bytes 73736 | tf_op jit(solution)/shard_map/ppermute | solution.py:12
  189.2 25.0 %collective-permute-start.41 = (bf16[48,256]{1,0:T(8,128)(2,1)S(1)}, bf16[48,256]{1,0:T(8,128)(2,1)S(1)}, u32[]{:S(2)}, u32[]{:S(2)}) collective-permute-start(bf16[48,256]{1,0:T(8,128)(2,1)S(1)} %get-tuple-element.5), channel_id=1, source_target_pairs={{1,0},{2,1},{3,2},{4,3},{5,4},{6,5},{7,6},{9,8},{10,9},{11,10},{12... | collective-permute-start | bytes 73736 | tf_op jit(solution)/shard_map/ppermute | solution.py:12
  190.5 22.4 %collective-permute-start.40 = (bf16[48,256]{1,0:T(8,128)(2,1)S(1)}, bf16[48,256]{1,0:T(8,128)(2,1)S(1)}, u32[]{:S(2)}, u32[]{:S(2)}) collective-permute-start(bf16[48,256]{1,0:T(8,128)(2,1)S(1)} %get-tuple-element.6), channel_id=1, source_target_pairs={{0,1},{1,2},{2,3},{3,4},{4,5},{5,6},{6,7},{8,9},{9,10},{10,11},{11... | collective-permute-start | bytes 73736 | tf_op jit(solution)/shard_map/ppermute | solution.py:12
  195.4 16.3 %collective-permute-start.39 = (bf16[48,256]{1,0:T(8,128)(2,1)S(1)}, bf16[48,256]{1,0:T(8,128)(2,1)S(1)}, u32[]{:S(2)}, u32[]{:S(2)}) collective-permute-start(bf16[48,256]{1,0:T(8,128)(2,1)S(1)} %get-tuple-element.7), channel_id=1, source_target_pairs={{8,0},{16,8},{24,16},{9,1},{17,9},{25,17},{10,2},{18,10},{26,18},{... | collective-permute-start | bytes 73736 | tf_op jit(solution)/shard_map/ppermute | solution.py:12
  196.7 13.7 %collective-permute-start.38 = (bf16[48,256]{1,0:T(8,128)(2,1)S(1)}, bf16[48,256]{1,0:T(8,128)(2,1)S(1)}, u32[]{:S(2)}, u32[]{:S(2)}) collective-permute-start(bf16[48,256]{1,0:T(8,128)(2,1)S(1)} %get-tuple-element.8), channel_id=1, source_target_pairs={{0,8},{8,16},{16,24},{1,9},{9,17},{17,25},{2,10},{10,18},{18,26},{... | collective-permute-start | bytes 73736 | tf_op jit(solution)/shard_map/ppermute | solution.py:12
  (14 other events, 171.5 us)
where the time goes:
time: 220 us; the launch traced here: 218 us
  starting transfers between devices  133 us (60%)
  other arithmetic  48.6 us (22%)
  waiting for transfers between devices  17.9 us (8%)
  matrix products  16.5 us (8%)
    ppermute x42, starting transfers between devices, from_behind(): lax.ppermute(value, axis, [(source, source + steps) for source in range(l...  133 us
    unnamed x35, other arithmetic  40.1 us
    ppermute x42, waiting for transfers between devices, from_behind(): lax.ppermute(value, axis, [(source, source + steps) for source in range(l...  17.9 us
    dot_general x8, matrix products, shards(): jnp.dot(driven, square, preferred_element_type=jnp.float32)  16.5 us
    concatenate x7, other arithmetic, shards(): jnp.concatenate([received[index] * couple_gain[index] for index in range(...  8.54 us
  transfers between devices with their start and end apart: 42, of which 8 were waited for; matrix products, arithmetic and copies ran while one was open for 19% of the time, Pallas kernels for 0%

commit v1 on v0

v1 whole, which is shorter than its diff:
```python
import functools

import jax
import jax.numpy as jnp
from jax import lax
from jax.experimental import pallas as pl
from jax.experimental.pallas import tpu as pltpu
from jax.sharding import PartitionSpec as P

ITERS = 8
FACES = 6
AXES = ("row", "col", "height")
MESH = pl.DeviceIdType.MESH
GROUPS = ((0, 32), (32, 16))
STAGES = ((0, 1), (4, 5), (2, 3))
SEND_ORDER = (2, 3, 4, 5, 0, 1)


def kernel(sizes, face, z_hbm, src_hbm, gain_ref, out,
           z, src, driven, acc, send, recv, z_sem, src_sem, send_sem, recv_sem):
    pos = [lax.axis_index(name) for name in AXES]

    def neighbour(f):
        axis, up = f // 2, f % 2
        n = sizes[axis]
        ids = list(pos)
        ids[axis] = lax.rem(pos[axis] + (1 if up else n - 1), n)
        return tuple(ids)

    targets = [neighbour(f) for f in range(FACES)]
    exists = [
        pos[f // 2] < sizes[f // 2] - 1 if f % 2 else pos[f // 2] > 0 for f in range(FACES)
    ]

    def z_copy(f):
        return pltpu.make_async_copy(z_hbm.at[:, f * face:(f + 1) * face], z.at[f], z_sem.at[f])

    src_copy = pltpu.make_async_copy(src_hbm, src, src_sem)
    src_copy.start()
    for f in SEND_ORDER:
        z_copy(f).start()
    barrier = pltpu.get_barrier_semaphore()
    for f in range(FACES):

        @pl.when(exists[f])
        def _():
            pl.semaphore_signal(barrier, inc=1, device_id=targets[f], device_id_type=MESH)

        @pl.when(jnp.logical_not(exists[f]))
        def _():
            for slot in range(ITERS - 1):
                recv[slot, f] = jnp.zeros(recv.shape[2:], recv.dtype)

    gains = [gain_ref[f].astype(jnp.float32) for f in range(FACES)]

    def remote(slot, f, g):
        lo, rows = GROUPS[g]
        return pltpu.make_async_remote_copy(
            src_ref=send.at[slot, f, lo:lo + rows],
            dst_ref=recv.at[slot, f ^ 1, lo:lo + rows],
            send_sem=send_sem.at[slot, f, g],
            recv_sem=recv_sem.at[slot, f ^ 1, g],
            device_id=targets[f],
            device_id_type=MESH,
        )

    def arrival(slot, f, g):
        return remote(slot, f ^ 1, g)

    def emit(slot, f, g, value):
        lo, rows = GROUPS[g]
        send[slot, f, lo:lo + rows] = value.astype(jnp.bfloat16)

        @pl.when(exists[f])
        def _():
            remote(slot, f, g).start()

    src_copy.wait()
    for i, f in enumerate(SEND_ORDER):
        z_copy(f).wait()
        value = jnp.dot(src[...], z[f], preferred_element_type=jnp.float32)
        if i == 0:
            pl.semaphore_wait(barrier, sum(here.astype(jnp.int32) for here in exists))
        for g, (lo, rows) in enumerate(GROUPS):
            emit(0, f, g, value[lo:lo + rows])

    def accept(slot, g, finish):
        lo, rows = GROUPS[g]
        for s, faces in enumerate(STAGES):
            for f in faces:

                @pl.when(exists[f])
                def _():
                    arrival(slot, f, g).wait_recv()

                cols = slice(f * face, (f + 1) * face)
                driven[lo:lo + rows, cols] = (
                    recv[slot, f, lo:lo + rows].astype(jnp.float32) * gains[f]
                    + src[lo:lo + rows, cols].astype(jnp.float32)
                ).astype(jnp.bfloat16)
            k0, k1 = faces[0] * face, (faces[-1] + 1) * face
            for f in SEND_ORDER:
                part = jnp.dot(driven[lo:lo + rows, k0:k1], z[f, k0:k1], preferred_element_type=jnp.float32)
                if s > 0:
                    part = acc[f, lo:lo + rows] + part
                if s + 1 < len(STAGES):
                    acc[f, lo:lo + rows] = part
                else:
                    finish(f, part)

    def step(iteration, carry):
        for g in range(len(GROUPS)):
            accept(iteration - 1, g, lambda f, value: emit(iteration, f, g, value))
        for g in range(len(GROUPS)):
            for f in range(FACES):

                @pl.when(exists[f])
                def _():
                    remote(iteration - 1, f, g).wait_send()

        return carry

    lax.fori_loop(1, ITERS - 1, step, 0)

    def finish_last(g):
        lo, rows = GROUPS[g]

        def finish(f, value):
            out[lo:lo + rows, f * face:(f + 1) * face] = value.astype(jnp.bfloat16)

        return finish

    for g in range(len(GROUPS)):
        accept(ITERS - 2, g, finish_last(g))
    for g in range(len(GROUPS)):
        for f in range(FACES):

            @pl.when(exists[f])
            def _():
                remote(ITERS - 2, f, g).wait_send()


def solution(mesh):
    sizes = tuple(mesh.shape[name] for name in AXES)

    def shards(impedance, sources, coupling):
        square = impedance[0, 0, 0]
        excite = sources[0, 0, 0]
        gain = coupling[0, 0, 0]
        exc, order = excite.shape
        face = order // FACES
        groups = len(GROUPS)
        slots = ITERS - 1
        outgoing = pl.pallas_call(
            functools.partial(kernel, sizes, face),
            out_shape=pltpu.VMEM((exc, order), jnp.bfloat16),
            in_specs=[
                pl.BlockSpec(memory_space=pl.ANY),
                pl.BlockSpec(memory_space=pl.ANY),
                pl.BlockSpec(memory_space=pltpu.SMEM),
            ],
            out_specs=pl.BlockSpec(memory_space=pltpu.VMEM),
            scratch_shapes=[
                pltpu.VMEM((FACES, order, face), jnp.bfloat16),
                pltpu.VMEM((exc, order), jnp.bfloat16),
                pltpu.VMEM((exc, order), jnp.bfloat16),
                pltpu.VMEM((FACES, exc, face), jnp.float32),
                pltpu.VMEM((slots, FACES, exc, face), jnp.bfloat16),
                pltpu.VMEM((slots, FACES, exc, face), jnp.bfloat16),
                pltpu.SemaphoreType.DMA((FACES,)),
                pltpu.SemaphoreType.DMA,
                pltpu.SemaphoreType.DMA((slots, FACES, groups)),
                pltpu.SemaphoreType.DMA((slots, FACES, groups)),
            ],
            compiler_params=pltpu.CompilerParams(
                collective_id=0, has_side_effects=True, vmem_limit_bytes=60 * 1024 * 1024
            ),
        )(square, excite, gain)
        return outgoing[None, None, None]

    placed = (
        P("row", "col", "height", None, None),
        P("row", "col", "height", None, None),
        P("row", "col", "height", None),
    )
    return jax.shard_map(
        shards,
        mesh=mesh,
        in_specs=placed,
        out_specs=P("row", "col", "height", None, None),
        check_vma=False,
    )
```

time: 220 us -> 46.8 us (0.21)
  the two profiles are of different devices: /device:TPU:25 before, /device:TPU:31 now
where the time goes in v1:
time: 46.8 us; the launch traced here: 46.7 us
  Pallas kernels  46 us (98%)
  local copies, waits for them, and re-layouts  0.66 us (1%)
    pallas_call x1, Pallas kernels, shards(): pl.pallas_call(functools.partial(kernel, sizes, face), out_shape=pltpu.VM...  46 us

profile of v1, /device:TPU:31, one launch (start us, length us, event | category | flops | bytes accessed | tf_op | source)
XLA Modules:
  0.0 46.7 jit_solution(17252466411523342978)
XLA Ops:
  0.0 46.0 %shard_map.37 = bf16[48,1536]{1,0:T(8,128)(2,1)S(1)} custom-call(bf16[1536,1536]{1,0:T(8,128)(2,1)} %bitcast.5, bf16[48,1536]{1,0:T(8,128)(2,1)} %bitcast.6, s32[6]{0:T(128)} %bitcast.7), custom_call_target="tpu_custom_call" | custom-call | tf_op jit(solution)/shard_map/pallas_call | solution.py:154
  46.0 0.7 %copy.5 = bf16[1,1,1,48,1536]{4,3,2,1,0:T(8,128)(2,1)} copy(bf16[1,1,1,48,1536]{4,3,2,1,0:T(8,128)(2,1)S(1)} %bitcast.4) | data formatting | bytes 294912

commit v2 on v1

v2 whole, which is shorter than its diff:
```python
import functools

import jax
import jax.numpy as jnp
from jax import lax
from jax.experimental import pallas as pl
from jax.experimental.pallas import tpu as pltpu
from jax.sharding import PartitionSpec as P

ITERS = 8
FACES = 6
AXES = ("row", "col", "height")
MESH = pl.DeviceIdType.MESH
GROUPS = ((0, 32), (32, 16))
STAGES = ((0, 2), (2, 6))
BATCHES = ((2, 3), (4, 5), (0, 1))
SEND_ORDER = sum(BATCHES, ())


def kernel(sizes, face, z_hbm, src_hbm, gain_ref, out,
           z, src, acc, zero, send, recv, z_sem, src_sem, send_sem, recv_sem):
    pos = [lax.axis_index(name) for name in AXES]

    def neighbour(f):
        axis, up = f // 2, f % 2
        n = sizes[axis]
        ids = list(pos)
        ids[axis] = lax.rem(pos[axis] + (1 if up else n - 1), n)
        return tuple(ids)

    targets = [neighbour(f) for f in range(FACES)]
    exists = [
        pos[f // 2] < sizes[f // 2] - 1 if f % 2 else pos[f // 2] > 0 for f in range(FACES)
    ]

    def z_copy(f):
        return pltpu.make_async_copy(z_hbm.at[:, f * face:(f + 1) * face], z.at[f], z_sem.at[f])

    src_copy = pltpu.make_async_copy(src_hbm, src, src_sem)
    src_copy.start()
    for f in SEND_ORDER:
        z_copy(f).start()
    barrier = pltpu.get_barrier_semaphore()
    for f in range(FACES):

        @pl.when(exists[f])
        def _():
            pl.semaphore_signal(barrier, inc=1, device_id=targets[f], device_id_type=MESH)

    zero[...] = jnp.zeros_like(zero)
    gains = [gain_ref[f].astype(jnp.float32) for f in range(FACES)]

    def remote(slot, f, g):
        rows = slice(GROUPS[g][0], sum(GROUPS[g]))
        return pltpu.make_async_remote_copy(
            src_ref=send.at[slot, f, rows],
            dst_ref=recv.at[slot, f ^ 1, rows],
            send_sem=send_sem.at[f],
            recv_sem=recv_sem.at[slot, g, 0 if f < STAGES[0][1] else 1],
            device_id=targets[f],
            device_id_type=MESH,
        )

    def launch(slot, f, g):
        rows = slice(GROUPS[g][0], sum(GROUPS[g]))

        @pl.when(exists[f])
        def _():
            remote(slot, f, g).start()

        @pl.when(jnp.logical_not(exists[f]))
        def _():
            pltpu.make_async_copy(
                zero.at[rows], recv.at[slot, f, rows], recv_sem.at[slot, g, 0 if f < STAGES[0][1] else 1]
            ).start()

    def arrived(slot, g, stage):
        rows = slice(GROUPS[g][0], sum(GROUPS[g]))
        whole = recv.at[slot, slice(*STAGES[stage]), rows]
        pltpu.make_async_copy(whole, whole, recv_sem.at[slot, g, stage]).wait()

    src_copy.wait()
    for i, f in enumerate(SEND_ORDER):
        z_copy(f).wait()
        value = jnp.dot(src[...], z[f], preferred_element_type=jnp.float32)
        send[0, f] = value.astype(jnp.bfloat16)
        if i == 0:
            pl.semaphore_wait(barrier, sum(here.astype(jnp.int32) for here in exists))
        for g in range(len(GROUPS)):
            launch(0, f, g)

    def driven(slot, g, stage):
        rows = slice(GROUPS[g][0], sum(GROUPS[g]))
        arrived(slot, g, stage)
        return jnp.concatenate(
            [
                (
                    recv[slot, f, rows].astype(jnp.float32) * gains[f]
                    + src[rows, f * face:(f + 1) * face].astype(jnp.float32)
                ).astype(jnp.bfloat16)
                for f in range(*STAGES[stage])
            ],
            axis=1,
        )

    def accept(slot, g, finish):
        rows = slice(GROUPS[g][0], sum(GROUPS[g]))
        first, second = (slice(lo * face, hi * face) for lo, hi in STAGES)
        part = driven(slot, g, 0)
        for f in SEND_ORDER:
            acc[f, rows] = jnp.dot(part, z[f, first], preferred_element_type=jnp.float32)
        rest = driven(slot, g, 1)
        for batch in BATCHES:
            values = [
                (acc[f, rows] + jnp.dot(rest, z[f, second], preferred_element_type=jnp.float32)).astype(jnp.bfloat16)
                for f in batch
            ]
            finish(rows, batch, values)

    def step(iteration, carry):
        for g in range(len(GROUPS)):

            def finish(rows, batch, values):
                for f, value in zip(batch, values):
                    send[iteration, f, rows] = value
                for f in batch:
                    launch(iteration, f, g)

            accept(iteration - 1, g, finish)
        return carry

    lax.fori_loop(1, ITERS - 1, step, 0)

    def finish_last(rows, batch, values):
        for f, value in zip(batch, values):
            out[rows, f * face:(f + 1) * face] = value

    for g in range(len(GROUPS)):
        accept(ITERS - 2, g, finish_last)
    for f in range(FACES):

        @pl.when(exists[f])
        def _():
            whole = send.at[:, f]
            pltpu.make_async_copy(whole, whole, send_sem.at[f]).wait()


def solution(mesh):
    sizes = tuple(mesh.shape[name] for name in AXES)

    def shards(impedance, sources, coupling):
        square = impedance[0, 0, 0]
        excite = sources[0, 0, 0]
        gain = coupling[0, 0, 0]
        exc, order = excite.shape
        face = order // FACES
        slots = ITERS - 1
        outgoing = pl.pallas_call(
            functools.partial(kernel, sizes, face),
            out_shape=pltpu.VMEM((exc, order), jnp.bfloat16),
            in_specs=[
                pl.BlockSpec(memory_space=pl.ANY),
                pl.BlockSpec(memory_space=pl.ANY),
                pl.BlockSpec(memory_space=pltpu.SMEM),
            ],
            out_specs=pl.BlockSpec(memory_space=pltpu.VMEM),
            scratch_shapes=[
                pltpu.VMEM((FACES, order, face), jnp.bfloat16),
                pltpu.VMEM((exc, order), jnp.bfloat16),
                pltpu.VMEM((FACES, exc, face), jnp.float32),
                pltpu.VMEM((exc, face), jnp.bfloat16),
                pltpu.VMEM((slots, FACES, exc, face), jnp.bfloat16),
                pltpu.VMEM((slots, FACES, exc, face), jnp.bfloat16),
                pltpu.SemaphoreType.DMA((FACES,)),
                pltpu.SemaphoreType.DMA,
                pltpu.SemaphoreType.DMA((FACES,)),
                pltpu.SemaphoreType.DMA((slots, len(GROUPS), len(STAGES))),
            ],
            compiler_params=pltpu.CompilerParams(
                collective_id=0, has_side_effects=True, vmem_limit_bytes=60 * 1024 * 1024
            ),
        )(square, excite, gain)
        return outgoing[None, None, None]

    placed = (
        P("row", "col", "height", None, None),
        P("row", "col", "height", None, None),
        P("row", "col", "height", None),
    )
    return jax.shard_map(
        shards,
        mesh=mesh,
        in_specs=placed,
        out_specs=P("row", "col", "height", None, None),
        check_vma=False,
    )
```

time: 46.8 us -> 43.8 us (0.936)
  the two profiles are of different devices: /device:TPU:31 before, /device:TPU:6 now
where the time goes in v2:
time: 43.8 us; the launch traced here: 43 us
  Pallas kernels  42.3 us (97%)
  local copies, waits for them, and re-layouts  0.66 us (2%)
    pallas_call x1, Pallas kernels, shards(): pl.pallas_call(functools.partial(kernel, sizes, face), out_shape=pltpu.VM...  42.3 us

profile of v2, /device:TPU:6, one launch (start us, length us, event | category | flops | bytes accessed | tf_op | source)
XLA Modules:
  0.0 43.0 jit_solution(11836484752364391733)
XLA Ops:
  0.0 42.3 %shard_map.37 = bf16[48,1536]{1,0:T(8,128)(2,1)S(1)} custom-call(bf16[1536,1536]{1,0:T(8,128)(2,1)} %bitcast.5, bf16[48,1536]{1,0:T(8,128)(2,1)} %bitcast.6, s32[6]{0:T(128)} %bitcast.7), custom_call_target="tpu_custom_call" | custom-call | tf_op jit(solution)/shard_map/pallas_call | solution.py:158
  42.3 0.7 %copy.5 = bf16[1,1,1,48,1536]{4,3,2,1,0:T(8,128)(2,1)} copy(bf16[1,1,1,48,1536]{4,3,2,1,0:T(8,128)(2,1)S(1)} %bitcast.4) | data formatting | bytes 294912

commit v3 on v2

--- a/solution.py
+++ b/solution.py
@@ -11,7 +11,7 @@
 FACES = 6
 AXES = ("row", "col", "height")
 MESH = pl.DeviceIdType.MESH
-GROUPS = ((0, 32), (32, 16))
+GROUPS = ((0, 16), (16, 16), (32, 16))
 STAGES = ((0, 2), (2, 6))
 BATCHES = ((2, 3), (4, 5), (0, 1))
 SEND_ORDER = sum(BATCHES, ())

time: 43.8 us -> 43.6 us (level)
  the two profiles are of different devices: /device:TPU:6 before, /device:TPU:31 now
where the time goes in v3:
time: 43.6 us; the launch traced here: 43.5 us
  Pallas kernels  42.8 us (98%)
  local copies, waits for them, and re-layouts  0.66 us (2%)
    pallas_call x1, Pallas kernels, shards(): pl.pallas_call(functools.partial(kernel, sizes, face), out_shape=pltpu.VM...  42.8 us

profile of v3, /device:TPU:31, one launch (start us, length us, event | category | flops | bytes accessed | tf_op | source)
XLA Modules:
  0.0 43.5 jit_solution(8563723135984009294)
XLA Ops:
  0.0 42.8 %shard_map.37 = bf16[48,1536]{1,0:T(8,128)(2,1)S(1)} custom-call(bf16[1536,1536]{1,0:T(8,128)(2,1)} %bitcast.5, bf16[48,1536]{1,0:T(8,128)(2,1)} %bitcast.6, s32[6]{0:T(128)} %bitcast.7), custom_call_target="tpu_custom_call" | custom-call | tf_op jit(solution)/shard_map/pallas_call | solution.py:158
  42.8 0.7 %copy.5 = bf16[1,1,1,48,1536]{4,3,2,1,0:T(8,128)(2,1)} copy(bf16[1,1,1,48,1536]{4,3,2,1,0:T(8,128)(2,1)S(1)} %bitcast.4) | data formatting | bytes 294912

commit v4 on v3

v4 whole, which is shorter than its diff:
```python
import functools

import jax
import jax.numpy as jnp
from jax import lax
from jax.experimental import pallas as pl
from jax.experimental.pallas import tpu as pltpu
from jax.sharding import PartitionSpec as P

ITERS = 8
FACES = 6
AXES = ("row", "col", "height")
MESH = pl.DeviceIdType.MESH
GROUPS = ((0, 16), (16, 16), (32, 16))
STAGES = ((0, 2), (1,))
BATCHES = ((2, 3), (4, 5, 0, 1))
SEND_ORDER = sum(BATCHES, ())


def kernel(sizes, face, z_hbm, src_hbm, gain_ref, out,
           z, src, acc, send, recv, z_sem, src_sem, send_sem, recv_sem):
    pos = [lax.axis_index(name) for name in AXES]

    def partner(f):
        axis, up = f // 2, f % 2
        n = sizes[axis]
        here = (pos[axis] < n - 1 if up else pos[axis] > 0).astype(jnp.int32)
        ids = list(pos)
        if axis == 0:
            ids[0] = lax.rem(pos[0] + (1 if up else n - 1), n)
            return tuple(ids), f ^ 1, here
        ids[axis] = pos[axis] + here * (1 if up else -1)
        ids[0] = pos[0] + (1 - here) * (1 - 2 * lax.rem(pos[0], 2))
        return tuple(ids), f + here * (-1 if up else 1), here

    partners = [partner(f) for f in range(FACES)]

    def z_copy(f):
        return pltpu.make_async_copy(z_hbm.at[:, f * face:(f + 1) * face], z.at[f], z_sem.at[f])

    src_copy = pltpu.make_async_copy(src_hbm, src, src_sem)
    src_copy.start()
    for f in SEND_ORDER:
        z_copy(f).start()
    barrier = pltpu.get_barrier_semaphore()
    for f in range(FACES):
        pl.semaphore_signal(barrier, inc=1, device_id=partners[f][0], device_id_type=MESH)
    gains = [(gain_ref[f] * partners[f][2]).astype(jnp.float32) for f in range(FACES)]

    def launch(slot, f, g):
        rows = slice(GROUPS[g][0], sum(GROUPS[g]))
        device, landing, _ = partners[f]
        pltpu.make_async_remote_copy(
            src_ref=send.at[slot, f, rows],
            dst_ref=recv.at[slot, landing, rows],
            send_sem=send_sem.at[f],
            recv_sem=recv_sem.at[slot, g, f // 2],
            device_id=device,
            device_id_type=MESH,
        ).start()

    def arrived(slot, g, axis):
        rows = slice(GROUPS[g][0], sum(GROUPS[g]))
        whole = recv.at[slot, 2 * axis:2 * axis + 2, rows]
        pltpu.make_async_copy(whole, whole, recv_sem.at[slot, g, axis]).wait()

    src_copy.wait()
    for i, f in enumerate(SEND_ORDER):
        z_copy(f).wait()
        value = jnp.dot(src[...], z[f], preferred_element_type=jnp.float32)
        send[0, f] = value.astype(jnp.bfloat16)
        if i == 0:
            pl.semaphore_wait(barrier, FACES)
        for g in range(len(GROUPS)):
            launch(0, f, g)

    def driven(slot, g, stage):
        rows = slice(GROUPS[g][0], sum(GROUPS[g]))
        for axis in STAGES[stage]:
            arrived(slot, g, axis)
        return [
            jnp.concatenate(
                [
                    (
                        recv[slot, f, rows].astype(jnp.float32) * gains[f]
                        + src[rows, f * face:(f + 1) * face].astype(jnp.float32)
                    ).astype(jnp.bfloat16)
                    for f in (2 * axis, 2 * axis + 1)
                ],
                axis=1,
            )
            for axis in STAGES[stage]
        ]

    def times(parts, stage, f):
        return sum(
            jnp.dot(part, z[f, 2 * axis * face:(2 * axis + 2) * face], preferred_element_type=jnp.float32)
            for part, axis in zip(parts, STAGES[stage])
        )

    def accept(slot, g, finish):
        rows = slice(GROUPS[g][0], sum(GROUPS[g]))
        last = len(STAGES) - 1
        for stage in range(last):
            parts = driven(slot, g, stage)
            for f in SEND_ORDER:
                total = times(parts, stage, f)
                acc[f, rows] = total if stage == 0 else acc[f, rows] + total
        parts = driven(slot, g, last)
        for batch in BATCHES:
            finish(rows, batch, [(acc[f, rows] + times(parts, last, f)).astype(jnp.bfloat16) for f in batch])

    def step(iteration, carry):
        for g in range(len(GROUPS)):

            def finish(rows, batch, values):
                for f, value in zip(batch, values):
                    send[iteration, f, rows] = value
                for f in batch:
                    launch(iteration, f, g)

            accept(iteration - 1, g, finish)
        return carry

    lax.fori_loop(1, ITERS - 1, step, 0)

    def finish_last(rows, batch, values):
        for f, value in zip(batch, values):
            out[rows, f * face:(f + 1) * face] = value

    for g in range(len(GROUPS)):
        accept(ITERS - 2, g, finish_last)
    for f in range(FACES):
        whole = send.at[:, f]
        pltpu.make_async_copy(whole, whole, send_sem.at[f]).wait()


def solution(mesh):
    sizes = tuple(mesh.shape[name] for name in AXES)

    def shards(impedance, sources, coupling):
        square = impedance[0, 0, 0]
        excite = sources[0, 0, 0]
        gain = coupling[0, 0, 0]
        exc, order = excite.shape
        face = order // FACES
        slots = ITERS - 1
        outgoing = pl.pallas_call(
            functools.partial(kernel, sizes, face),
            out_shape=pltpu.VMEM((exc, order), jnp.bfloat16),
            in_specs=[
                pl.BlockSpec(memory_space=pl.ANY),
                pl.BlockSpec(memory_space=pl.ANY),
                pl.BlockSpec(memory_space=pltpu.SMEM),
            ],
            out_specs=pl.BlockSpec(memory_space=pltpu.VMEM),
            scratch_shapes=[
                pltpu.VMEM((FACES, order, face), jnp.bfloat16),
                pltpu.VMEM((exc, order), jnp.bfloat16),
                pltpu.VMEM((FACES, exc, face), jnp.float32),
                pltpu.VMEM((slots, FACES, exc, face), jnp.bfloat16),
                pltpu.VMEM((slots, FACES, exc, face), jnp.bfloat16),
                pltpu.SemaphoreType.DMA((FACES,)),
                pltpu.SemaphoreType.DMA,
                pltpu.SemaphoreType.DMA((FACES,)),
                pltpu.SemaphoreType.DMA((slots, len(GROUPS), len(AXES))),
            ],
            compiler_params=pltpu.CompilerParams(
                collective_id=0, has_side_effects=True, vmem_limit_bytes=60 * 1024 * 1024
            ),
        )(square, excite, gain)
        return outgoing[None, None, None]

    placed = (
        P("row", "col", "height", None, None),
        P("row", "col", "height", None, None),
        P("row", "col", "height", None),
    )
    return jax.shard_map(
        shards,
        mesh=mesh,
        in_specs=placed,
        out_specs=P("row", "col", "height", None, None),
        check_vma=False,
    )
```

time: 43.6 us -> 44.4 us (1.018)
  the two profiles are of different devices: /device:TPU:31 before, /device:TPU:6 now
where the time goes in v4:
time: 44.4 us; the launch traced here: 44.3 us
  Pallas kernels  43.6 us (98%)
  local copies, waits for them, and re-layouts  0.66 us (1%)
    pallas_call x1, Pallas kernels, shards(): pl.pallas_call(functools.partial(kernel, sizes, face), out_shape=pltpu.VM...  43.6 us

profile of v4, /device:TPU:6, one launch (start us, length us, event | category | flops | bytes accessed | tf_op | source)
XLA Modules:
  0.0 44.3 jit_solution(11006680494720376077)
XLA Ops:
  0.0 43.6 %shard_map.37 = bf16[48,1536]{1,0:T(8,128)(2,1)S(1)} custom-call(bf16[1536,1536]{1,0:T(8,128)(2,1)} %bitcast.5, bf16[48,1536]{1,0:T(8,128)(2,1)} %bitcast.6, s32[6]{0:T(128)} %bitcast.7), custom_call_target="tpu_custom_call" | custom-call | tf_op jit(solution)/shard_map/pallas_call | solution.py:148
  43.6 0.7 %copy.5 = bf16[1,1,1,48,1536]{4,3,2,1,0:T(8,128)(2,1)} copy(bf16[1,1,1,48,1536]{4,3,2,1,0:T(8,128)(2,1)S(1)} %bitcast.4) | data formatting | bytes 294912

commit v5 on v4

v5 whole, which is shorter than its diff:
```python
import functools

import jax
import jax.numpy as jnp
from jax import lax
from jax.experimental import pallas as pl
from jax.experimental.pallas import tpu as pltpu
from jax.sharding import PartitionSpec as P

ITERS = 8
FACES = 6
AXES = ("row", "col", "height")
MESH = pl.DeviceIdType.MESH
ROWS = 16
STAGES = ((0, 2), (2, 6))
BATCHES = ((2, 3), (4, 5), (0, 1))
SEND_ORDER = sum(BATCHES, ())


def kernel(sizes, face, z_hbm, src_hbm, gain_ref, out,
           z, src, acc, send, recv, z_sem, src_sem, send_sem, recv_sem):
    chains = src.shape[0]
    pos = [lax.axis_index(name) for name in AXES]

    def partner(f):
        axis, up = f // 2, f % 2
        n = sizes[axis]
        here = (pos[axis] < n - 1 if up else pos[axis] > 0).astype(jnp.int32)
        ids = list(pos)
        if axis == 0:
            ids[0] = lax.rem(pos[0] + (1 if up else n - 1), n)
            return tuple(ids), f ^ 1, here
        ids[axis] = pos[axis] + here * (1 if up else -1)
        ids[0] = pos[0] + (1 - here) * (1 - 2 * lax.rem(pos[0], 2))
        return tuple(ids), f + here * (-1 if up else 1), here

    partners = [partner(f) for f in range(FACES)]

    def z_copy(f):
        return pltpu.make_async_copy(z_hbm.at[:, f * face:(f + 1) * face], z.at[f], z_sem.at[f])

    def src_copy(g):
        return pltpu.make_async_copy(src_hbm.at[g * ROWS:(g + 1) * ROWS], src.at[g], src_sem.at[g])

    for g in range(chains):
        src_copy(g).start()
    for f in SEND_ORDER:
        z_copy(f).start()
    barrier = pltpu.get_barrier_semaphore()
    for f in range(FACES):
        pl.semaphore_signal(barrier, inc=1, device_id=partners[f][0], device_id_type=MESH)
    gains = [(gain_ref[f] * partners[f][2]).astype(jnp.float32) for f in range(FACES)]

    def launch(slot, f, g):
        device, landing, _ = partners[f]
        pltpu.make_async_remote_copy(
            src_ref=send.at[slot, g, f],
            dst_ref=recv.at[slot, g, landing],
            send_sem=send_sem.at[f],
            recv_sem=recv_sem.at[slot, g, 0 if f < STAGES[0][1] else 1],
            device_id=device,
            device_id_type=MESH,
        ).start()

    for g in range(chains):
        src_copy(g).wait()
    for i, f in enumerate(SEND_ORDER):
        z_copy(f).wait()
        value = jnp.dot(src[...].reshape(chains * ROWS, -1), z[f], preferred_element_type=jnp.float32)
        for g in range(chains):
            send[0, g, f] = value[g * ROWS:(g + 1) * ROWS].astype(jnp.bfloat16)
        if i == 0:
            pl.semaphore_wait(barrier, FACES)
        for g in range(chains):
            launch(0, f, g)

    def driven(slot, g, stage):
        whole = recv.at[slot, g, slice(*STAGES[stage])]
        pltpu.make_async_copy(whole, whole, recv_sem.at[slot, g, stage]).wait()
        return jnp.concatenate(
            [
                (
                    recv[slot, g, f].astype(jnp.float32) * gains[f]
                    + src[g, :, f * face:(f + 1) * face].astype(jnp.float32)
                ).astype(jnp.bfloat16)
                for f in range(*STAGES[stage])
            ],
            axis=1,
        )

    first, second = (slice(lo * face, hi * face) for lo, hi in STAGES)

    def step(iteration, carry):
        def chain(g, carry):
            part = driven(iteration - 1, g, 0)
            for f in SEND_ORDER:
                acc[f] = jnp.dot(part, z[f, first], preferred_element_type=jnp.float32)
            rest = driven(iteration - 1, g, 1)
            for batch in BATCHES:
                for f in batch:
                    total = acc[f] + jnp.dot(rest, z[f, second], preferred_element_type=jnp.float32)
                    send[iteration, g, f] = total.astype(jnp.bfloat16)

                @pl.when(iteration < ITERS - 1)
                def _():
                    for f in batch:
                        launch(iteration, f, g)

            return carry

        return lax.fori_loop(0, chains, chain, carry)

    lax.fori_loop(1, ITERS, step, 0)

    for g in range(chains):
        for f in range(FACES):
            out[g * ROWS:(g + 1) * ROWS, f * face:(f + 1) * face] = send[ITERS - 1, g, f]
    for f in range(FACES):
        whole = send.at[0:ITERS - 1, :, f]
        pltpu.make_async_copy(whole, whole, send_sem.at[f]).wait()


def solution(mesh):
    sizes = tuple(mesh.shape[name] for name in AXES)

    def shards(impedance, sources, coupling):
        square = impedance[0, 0, 0]
        excite = sources[0, 0, 0]
        gain = coupling[0, 0, 0]
        exc, order = excite.shape
        face = order // FACES
        chains = exc // ROWS
        outgoing = pl.pallas_call(
            functools.partial(kernel, sizes, face),
            out_shape=pltpu.VMEM((exc, order), jnp.bfloat16),
            in_specs=[
                pl.BlockSpec(memory_space=pl.ANY),
                pl.BlockSpec(memory_space=pl.ANY),
                pl.BlockSpec(memory_space=pltpu.SMEM),
            ],
            out_specs=pl.BlockSpec(memory_space=pltpu.VMEM),
            scratch_shapes=[
                pltpu.VMEM((FACES, order, face), jnp.bfloat16),
                pltpu.VMEM((chains, ROWS, order), jnp.bfloat16),
                pltpu.VMEM((FACES, ROWS, face), jnp.float32),
                pltpu.VMEM((ITERS, chains, FACES, ROWS, face), jnp.bfloat16),
                pltpu.VMEM((ITERS - 1, chains, FACES, ROWS, face), jnp.bfloat16),
                pltpu.SemaphoreType.DMA((FACES,)),
                pltpu.SemaphoreType.DMA((chains,)),
                pltpu.SemaphoreType.DMA((FACES,)),
                pltpu.SemaphoreType.DMA((ITERS - 1, chains, len(STAGES))),
            ],
            compiler_params=pltpu.CompilerParams(
                collective_id=0, has_side_effects=True, vmem_limit_bytes=60 * 1024 * 1024
            ),
        )(square, excite, gain)
        return outgoing[None, None, None]

    placed = (
        P("row", "col", "height", None, None),
        P("row", "col", "height", None, None),
        P("row", "col", "height", None),
    )
    return jax.shard_map(
        shards,
        mesh=mesh,
        in_specs=placed,
        out_specs=P("row", "col", "height", None, None),
        check_vma=False,
    )
```

time: 44.4 us -> 43.5 us (0.980)
  Pallas kernels: 43.6 us -> 42.7 us
    pallas_call x1, Pallas kernels: 43.6 us -> 42.7 us  [shards(): pl.pallas_call(functools.partial(kernel, sizes, face), out_shape=pltpu.VM...]
where the time goes in v5:
time: 43.5 us; the launch traced here: 43.4 us
  Pallas kernels  42.7 us (98%)
  local copies, waits for them, and re-layouts  0.66 us (2%)
    pallas_call x1, Pallas kernels, shards(): pl.pallas_call(functools.partial(kernel, sizes, face), out_shape=pltpu.VM...  42.7 us

profile of v5, /device:TPU:6, one launch (start us, length us, event | category | flops | bytes accessed | tf_op | source)
XLA Modules:
  0.0 43.4 jit_solution(2534076422911087458)
XLA Ops:
  0.0 42.7 %shard_map.37 = bf16[48,1536]{1,0:T(8,128)(2,1)S(1)} custom-call(bf16[1536,1536]{1,0:T(8,128)(2,1)} %bitcast.5, bf16[48,1536]{1,0:T(8,128)(2,1)} %bitcast.6, s32[6]{0:T(128)} %bitcast.7), custom_call_target="tpu_custom_call" | custom-call | tf_op jit(solution)/shard_map/pallas_call | solution.py:133
  42.7 0.7 %copy.5 = bf16[1,1,1,48,1536]{4,3,2,1,0:T(8,128)(2,1)} copy(bf16[1,1,1,48,1536]{4,3,2,1,0:T(8,128)(2,1)S(1)} %bitcast.4) | data formatting | bytes 294912

commit v6 on v5

--- a/solution.py
+++ b/solution.py
@@ -51,28 +51,36 @@
         pl.semaphore_signal(barrier, inc=1, device_id=partners[f][0], device_id_type=MESH)
     gains = [(gain_ref[f] * partners[f][2]).astype(jnp.float32) for f in range(FACES)]
 
+    swap = lax.rem(pos[0], 2)
+
     def launch(slot, f, g):
-        device, landing, _ = partners[f]
+        (device, landing, _), (other, other_landing, _) = partners[f], partners[f ^ 1]
+        device = tuple(a + swap * (b - a) for a, b in zip(device, other))
+        landing = landing + swap * (other_landing - landing)
+        stage = 0 if f < STAGES[0][1] else 1
+        f = f + swap * (1 - 2 * (f % 2))
         pltpu.make_async_remote_copy(
             src_ref=send.at[slot, g, f],
             dst_ref=recv.at[slot, g, landing],
             send_sem=send_sem.at[f],
-            recv_sem=recv_sem.at[slot, g, 0 if f < STAGES[0][1] else 1],
+            recv_sem=recv_sem.at[slot, g, stage],
             device_id=device,
             device_id_type=MESH,
         ).start()
 
     for g in range(chains):
         src_copy(g).wait()
-    for i, f in enumerate(SEND_ORDER):
-        z_copy(f).wait()
-        value = jnp.dot(src[...].reshape(chains * ROWS, -1), z[f], preferred_element_type=jnp.float32)
-        for g in range(chains):
-            send[0, g, f] = value[g * ROWS:(g + 1) * ROWS].astype(jnp.bfloat16)
+    for i, batch in enumerate(BATCHES):
+        for f in batch:
+            z_copy(f).wait()
+            value = jnp.dot(src[...].reshape(chains * ROWS, -1), z[f], preferred_element_type=jnp.float32)
+            for g in range(chains):
+                send[0, g, f] = value[g * ROWS:(g + 1) * ROWS].astype(jnp.bfloat16)
         if i == 0:
             pl.semaphore_wait(barrier, FACES)
         for g in range(chains):
-            launch(0, f, g)
+            for f in batch:
+                launch(0, f, g)
 
     def driven(slot, g, stage):
         whole = recv.at[slot, g, slice(*STAGES[stage])]

time: 43.5 us -> 43.8 us (level)
  no operation moved by 1% of the time
where the time goes in v6:
time: 43.8 us; the launch traced here: 43.7 us
  Pallas kernels  43 us (98%)
  local copies, waits for them, and re-layouts  0.66 us (2%)
    pallas_call x1, Pallas kernels, shards(): pl.pallas_call(functools.partial(kernel, sizes, face), out_shape=pltpu.VM...  43 us

profile of v6, /device:TPU:6, one launch (start us, length us, event | category | flops | bytes accessed | tf_op | source)
XLA Modules:
  0.0 43.7 jit_solution(6332761340577237437)
XLA Ops:
  0.0 43.0 %shard_map.37 = bf16[48,1536]{1,0:T(8,128)(2,1)S(1)} custom-call(bf16[1536,1536]{1,0:T(8,128)(2,1)} %bitcast.5, bf16[48,1536]{1,0:T(8,128)(2,1)} %bitcast.6, s32[6]{0:T(128)} %bitcast.7), custom_call_target="tpu_custom_call" | custom-call | tf_op jit(solution)/shard_map/pallas_call | solution.py:141
  43.0 0.7 %copy.5 = bf16[1,1,1,48,1536]{4,3,2,1,0:T(8,128)(2,1)} copy(bf16[1,1,1,48,1536]{4,3,2,1,0:T(8,128)(2,1)S(1)} %bitcast.4) | data formatting | bytes 294912

commit v7 on v5

--- a/solution.py
+++ b/solution.py
@@ -17,8 +17,8 @@
 SEND_ORDER = sum(BATCHES, ())
 
 
-def kernel(sizes, face, z_hbm, src_hbm, gain_ref, out,
-           z, src, acc, send, recv, z_sem, src_sem, send_sem, recv_sem):
+def kernel(sizes, face, z_hbm, src_hbm, gain_hbm, out,
+           gain_ref, z, src, acc, send, recv, gain_sem, z_sem, src_sem, send_sem, recv_sem):
     chains = src.shape[0]
     pos = [lax.axis_index(name) for name in AXES]
 
@@ -42,14 +42,15 @@
     def src_copy(g):
         return pltpu.make_async_copy(src_hbm.at[g * ROWS:(g + 1) * ROWS], src.at[g], src_sem.at[g])
 
+    barrier = pltpu.get_barrier_semaphore()
+    for f in range(FACES):
+        pl.semaphore_signal(barrier, inc=1, device_id=partners[f][0], device_id_type=MESH)
     for g in range(chains):
         src_copy(g).start()
     for f in SEND_ORDER:
         z_copy(f).start()
-    barrier = pltpu.get_barrier_semaphore()
-    for f in range(FACES):
-        pl.semaphore_signal(barrier, inc=1, device_id=partners[f][0], device_id_type=MESH)
-    gains = [(gain_ref[f] * partners[f][2]).astype(jnp.float32) for f in range(FACES)]
+    gain_copy = pltpu.make_async_copy(gain_hbm, gain_ref, gain_sem)
+    gain_copy.start()
 
     def launch(slot, f, g):
         device, landing, _ = partners[f]
@@ -73,6 +74,9 @@
             pl.semaphore_wait(barrier, FACES)
         for g in range(chains):
             launch(0, f, g)
+
+    gain_copy.wait()
+    gains = [(gain_ref[f] * partners[f][2]).astype(jnp.float32) for f in range(FACES)]
 
     def driven(slot, g, stage):
         whole = recv.at[slot, g, slice(*STAGES[stage])]
@@ -136,15 +140,17 @@
             in_specs=[
                 pl.BlockSpec(memory_space=pl.ANY),
                 pl.BlockSpec(memory_space=pl.ANY),
-                pl.BlockSpec(memory_space=pltpu.SMEM),
+                pl.BlockSpec(memory_space=pl.ANY),
             ],
             out_specs=pl.BlockSpec(memory_space=pltpu.VMEM),
             scratch_shapes=[
+                pltpu.SMEM((FACES,), jnp.int32),
                 pltpu.VMEM((FACES, order, face), jnp.bfloat16),
                 pltpu.VMEM((chains, ROWS, order), jnp.bfloat16),
                 pltpu.VMEM((FACES, ROWS, face), jnp.float32),
                 pltpu.VMEM((ITERS, chains, FACES, ROWS, face), jnp.bfloat16),
                 pltpu.VMEM((ITERS - 1, chains, FACES, ROWS, face), jnp.bfloat16),
+                pltpu.SemaphoreType.DMA,
                 pltpu.SemaphoreType.DMA((FACES,)),
                 pltpu.SemaphoreType.DMA((chains,)),
                 pltpu.SemaphoreType.DMA((FACES,)),

time: 43.5 us -> 43 us (0.989)
  Pallas kernels: 42.7 us -> 42.2 us
    pallas_call x1, Pallas kernels: 42.7 us -> 42.2 us  [shards(): pl.pallas_call(functools.partial(kernel, sizes, face), out_shape=pltpu.VM...]
where the time goes in v7:
time: 43 us; the launch traced here: 42.9 us
  Pallas kernels  42.2 us (98%)
  local copies, waits for them, and re-layouts  0.66 us (2%)
    pallas_call x1, Pallas kernels, shards(): pl.pallas_call(functools.partial(kernel, sizes, face), out_shape=pltpu.VM...  42.2 us

profile of v7, /device:TPU:6, one launch (start us, length us, event | category | flops | bytes accessed | tf_op | source)
XLA Modules:
  0.0 42.9 jit_solution(15087488544025420383)
XLA Ops:
  0.0 42.2 %shard_map.37 = bf16[48,1536]{1,0:T(8,128)(2,1)S(1)} custom-call(bf16[1536,1536]{1,0:T(8,128)(2,1)} %bitcast.5, bf16[48,1536]{1,0:T(8,128)(2,1)} %bitcast.6, s32[6]{0:T(128)} %bitcast.7), custom_call_target="tpu_custom_call" | custom-call | tf_op jit(solution)/shard_map/pallas_call | solution.py:137
  42.2 0.7 %copy.5 = bf16[1,1,1,48,1536]{4,3,2,1,0:T(8,128)(2,1)} copy(bf16[1,1,1,48,1536]{4,3,2,1,0:T(8,128)(2,1)S(1)} %bitcast.4) | data formatting | bytes 294912

commit v8 on v7

--- a/solution.py
+++ b/solution.py
@@ -15,6 +15,7 @@
 STAGES = ((0, 2), (2, 6))
 BATCHES = ((2, 3), (4, 5), (0, 1))
 SEND_ORDER = sum(BATCHES, ())
+LOADS = 3
 
 
 def kernel(sizes, face, z_hbm, src_hbm, gain_hbm, out,
@@ -47,7 +48,7 @@
         pl.semaphore_signal(barrier, inc=1, device_id=partners[f][0], device_id_type=MESH)
     for g in range(chains):
         src_copy(g).start()
-    for f in SEND_ORDER:
+    for f in SEND_ORDER[:LOADS]:
         z_copy(f).start()
     gain_copy = pltpu.make_async_copy(gain_hbm, gain_ref, gain_sem)
     gain_copy.start()
@@ -67,6 +68,8 @@
         src_copy(g).wait()
     for i, f in enumerate(SEND_ORDER):
         z_copy(f).wait()
+        if i + LOADS < FACES:
+            z_copy(SEND_ORDER[i + LOADS]).start()
         value = jnp.dot(src[...].reshape(chains * ROWS, -1), z[f], preferred_element_type=jnp.float32)
         for g in range(chains):
             send[0, g, f] = value[g * ROWS:(g + 1) * ROWS].astype(jnp.bfloat16)

time: 43 us -> 42.8 us (level)
  no operation moved by 1% of the time
where the time goes in v8:
time: 42.8 us; the launch traced here: 42.6 us
  Pallas kernels  41.9 us (98%)
  local copies, waits for them, and re-layouts  0.66 us (2%)
    pallas_call x1, Pallas kernels, shards(): pl.pallas_call(functools.partial(kernel, sizes, face), out_shape=pltpu.VM...  41.9 us

profile of v8, /device:TPU:6, one launch (start us, length us, event | category | flops | bytes accessed | tf_op | source)
XLA Modules:
  0.0 42.6 jit_solution(15563293857050897068)
XLA Ops:
  0.0 41.9 %shard_map.37 = bf16[48,1536]{1,0:T(8,128)(2,1)S(1)} custom-call(bf16[1536,1536]{1,0:T(8,128)(2,1)} %bitcast.5, bf16[48,1536]{1,0:T(8,128)(2,1)} %bitcast.6, s32[6]{0:T(128)} %bitcast.7), custom_call_target="tpu_custom_call" | custom-call | tf_op jit(solution)/shard_map/pallas_call | solution.py:140
  41.9 0.7 %copy.5 = bf16[1,1,1,48,1536]{4,3,2,1,0:T(8,128)(2,1)} copy(bf16[1,1,1,48,1536]{4,3,2,1,0:T(8,128)(2,1)S(1)} %bitcast.4) | data formatting | bytes 294912

commit v9 on v8

--- a/solution.py
+++ b/solution.py
@@ -13,9 +13,9 @@
 MESH = pl.DeviceIdType.MESH
 ROWS = 16
 STAGES = ((0, 2), (2, 6))
-BATCHES = ((2, 3), (4, 5), (0, 1))
+BATCHES = ((4, 5), (2, 3), (0, 1))
 SEND_ORDER = sum(BATCHES, ())
-LOADS = 3
+LOADS = 2
 
 
 def kernel(sizes, face, z_hbm, src_hbm, gain_hbm, out,

time: 42.8 us -> 45 us (1.051)
  Pallas kernels: 41.9 us -> 44.2 us
    pallas_call x1, Pallas kernels: 41.9 us -> 44.2 us  [shards(): pl.pallas_call(functools.partial(kernel, sizes, face), out_shape=pltpu.VM...]
where the time goes in v9:
time: 45 us; the launch traced here: 44.8 us
  Pallas kernels  44.2 us (98%)
  local copies, waits for them, and re-layouts  0.66 us (1%)
    pallas_call x1, Pallas kernels, shards(): pl.pallas_call(functools.partial(kernel, sizes, face), out_shape=pltpu.VM...  44.2 us

profile of v9, /device:TPU:6, one launch (start us, length us, event | category | flops | bytes accessed | tf_op | source)
XLA Modules:
  0.0 44.8 jit_solution(6168121420894773582)
XLA Ops:
  0.0 44.2 %shard_map.37 = bf16[48,1536]{1,0:T(8,128)(2,1)S(1)} custom-call(bf16[1536,1536]{1,0:T(8,128)(2,1)} %bitcast.5, bf16[48,1536]{1,0:T(8,128)(2,1)} %bitcast.6, s32[6]{0:T(128)} %bitcast.7), custom_call_target="tpu_custom_call" | custom-call | tf_op jit(solution)/shard_map/pallas_call | solution.py:140
  44.2 0.7 %copy.5 = bf16[1,1,1,48,1536]{4,3,2,1,0:T(8,128)(2,1)} copy(bf16[1,1,1,48,1536]{4,3,2,1,0:T(8,128)(2,1)S(1)} %bitcast.4) | data formatting | bytes 294912
